TPU v7x, 32 devices: a whole 2x2x4 slice. The times are simulated.
32 devices in a mesh: stream: 2 (over y), seq: 8 (over z, core), tensor: 2 (over x).
Axes of the slice: x: 2, y: 2, z: 4, core: 2. Of those that a mesh axis runs over, the one named last changes fastest.
Arguments:
- hidden: bfloat16 [2, 1, 4096, 4096], P('stream', None, 'seq', 'tensor'), may hold values from -32 to 32
- norm_gain: float32 [4096], replicated, may hold values from 0.1 to 1.9
- query_weight: bfloat16 [4096, 4096], P('seq', 'tensor'), may hold values from -1 to 1
- key_weight: bfloat16 [4096, 1024], P('seq', 'tensor'), may hold values from -24 to 24
- value_projection_weight: bfloat16 [4096, 1024], P('seq', 'tensor'), may hold values from -0.09375 to 0.09375
- out_weight: bfloat16 [4096, 4096], P('tensor', 'seq'), may hold values from -0.125 to 0.125
Outputs:
- cross_out: bfloat16 [2, 1, 4096, 4096], P('stream', None, 'seq', 'tensor')
All inputs are finite; a program needn't handle non-finite values.
Results may differ from a plain program's by a relative error of at most 0.014.
The roundings to bfloat16 on the way count: a program that leaves them out, or rounds other values in their place, can miss the bound.
Values may be sent and summed in bfloat16 or wider, within the bound.
A program may use at most 256 MiB of HBM per device.

v0:
```python
import functools

import jax
import jax.numpy as jnp
from jax import lax
from jax.experimental import pallas as pl
from jax.experimental.pallas import tpu as pltpu
from jax.sharding import PartitionSpec as P

HEAD_DIM = 128
ROW_CHUNKS = 2
KEY_BLOCK = 1024
LOG2E = 1.4426950408889634


def swap_pairs(block, axis):
    count = lax.axis_size(axis)
    return lax.ppermute(block, axis, [(i, i ^ 1) for i in range(count)])


def attend_kernel(repeat, start_ref, q_ref, k_ref, v_ref, o_ref, m_ref, l_ref, acc_ref):
    step = pl.program_id(1)
    rows = q_ref.shape[0]
    keys = k_ref.shape[0]
    start = start_ref[0]
    last = (start + rows - 1) // keys
    scale = LOG2E * HEAD_DIM ** (-0.5)

    @pl.when(step == 0)
    def _():
        m_ref[...] = jnp.full_like(m_ref, -1e30)
        l_ref[...] = jnp.zeros_like(l_ref)
        acc_ref[...] = jnp.zeros_like(acc_ref)

    def update(masked):
        k = k_ref[...]
        v = v_ref[...]
        if masked:
            frame = start + lax.broadcasted_iota(jnp.int32, (keys, rows), 1)
            key = step * keys + lax.broadcasted_iota(jnp.int32, (keys, rows), 0)
            allowed = key <= frame

        def scored(r):
            q = q_ref[:, r * HEAD_DIM:(r + 1) * HEAD_DIM]
            return lax.dot_general(k, q, (((1,), (1,)), ((), ())), preferred_element_type=jnp.float32)

        following = scored(0)
        for r in range(repeat):
            s = following
            if r + 1 < repeat:
                following = scored(r + 1)
            if masked:
                s = jnp.where(allowed, s, -1e30)
            top = jnp.max(s, axis=0, keepdims=True) * scale
            before = m_ref[r]
            fresh = jnp.maximum(before, top)
            m_ref[r] = fresh
            alpha = jnp.exp2(before - fresh)
            p = jnp.exp2(s * scale - fresh)
            l_ref[r] = alpha * l_ref[r] + jnp.sum(p, axis=0, keepdims=True)
            acc_ref[r] = alpha * acc_ref[r] + lax.dot_general(
                v, p.astype(jnp.bfloat16), (((0,), (0,)), ((), ())), preferred_element_type=jnp.float32
            )

    @pl.when(step < last)
    def _():
        update(False)

    @pl.when(step == last)
    def _():
        update(True)
        for r in range(repeat):
            attended = (acc_ref[r] / l_ref[r]).T
            o_ref[:, r * HEAD_DIM:(r + 1) * HEAD_DIM] = attended.astype(o_ref.dtype)


def attend(start, queries, keys_values, repeat):
    rows, width = queries.shape
    count = keys_values.shape[0]
    groups = width // (repeat * HEAD_DIM)
    block = min(KEY_BLOCK, count)

    def at(step, start_ref):
        return jnp.minimum(step, (start_ref[0] + rows - 1) // block)

    return pl.pallas_call(
        functools.partial(attend_kernel, repeat),
        out_shape=jax.ShapeDtypeStruct((rows, width), jnp.bfloat16),
        grid_spec=pltpu.PrefetchScalarGridSpec(
            num_scalar_prefetch=1,
            grid=(groups, count // block),
            in_specs=[
                pl.BlockSpec((rows, repeat * HEAD_DIM), lambda g, i, s: (0, g)),
                pl.BlockSpec((block, HEAD_DIM), lambda g, i, s: (at(i, s), g)),
                pl.BlockSpec((block, HEAD_DIM), lambda g, i, s: (at(i, s), groups + g)),
            ],
            out_specs=pl.BlockSpec((rows, repeat * HEAD_DIM), lambda g, i, s: (0, g)),
            scratch_shapes=[
                pltpu.VMEM((repeat, 1, rows), jnp.float32),
                pltpu.VMEM((repeat, 1, rows), jnp.float32),
                pltpu.VMEM((repeat, HEAD_DIM, rows), jnp.float32),
            ],
        ),
        compiler_params=pltpu.CompilerParams(
            dimension_semantics=("arbitrary", "arbitrary"), vmem_limit_bytes=32 * 1024 * 1024
        ),
        cost_estimate=pl.CostEstimate(
            flops=8 * rows * count * width,
            bytes_accessed=2 * (2 * rows * width + keys_values.size),
            transcendentals=rows * count * width // HEAD_DIM,
        ),
    )(start.reshape(1), queries, keys_values, keys_values)


def y_share(mine, core, after=None):
    depth = mine.shape[0] // 2
    part = lax.dynamic_slice_in_dim(mine, core * depth, depth, 0)
    near = lax.ppermute(part, "stream", [(0, 1), (1, 0)])
    if after is None:
        return near, swap_pairs(near, "seq")
    near, after = lax.optimization_barrier((near, after))
    return near, swap_pairs(near, "seq"), after


def body(hidden, norm_gain, query_weight, key_weight, value_projection_weight, out_weight):
    windows, frame_count = hidden.shape[1], hidden.shape[2]
    n_tensor = lax.axis_size("tensor")
    n_seq = lax.axis_size("seq")
    stream = lax.axis_index("stream")
    tensor = lax.axis_index("tensor")
    seq = lax.axis_index("seq")
    core = seq % 2
    rows = windows * frame_count
    depth = query_weight.shape[0] // 2
    out_half = out_weight.shape[1] // 2

    kv_weight = jnp.concatenate([key_weight, value_projection_weight], axis=1)
    kv_mine = lax.all_gather(
        lax.dynamic_slice_in_dim(kv_weight, stream * depth, depth, 0), "seq", axis=0, tiled=True
    )
    query_mine = lax.all_gather(
        lax.dynamic_slice_in_dim(query_weight, stream * depth, depth, 0), "seq", axis=0, tiled=True
    )
    out_mine = lax.all_gather(
        lax.dynamic_slice_in_dim(out_weight, stream * out_half, out_half, 1), "seq", axis=1, tiled=True
    )

    local = hidden.reshape(rows, hidden.shape[3])
    if n_tensor == 2:
        other = lax.ppermute(local, "tensor", [(0, 1), (1, 0)])
        gathered = jnp.where(
            tensor == 0,
            jnp.concatenate([local, other], axis=1),
            jnp.concatenate([other, local], axis=1),
        )
    else:
        gathered = lax.all_gather(local, "tensor", axis=1, tiled=True)
    flat = gathered.astype(jnp.float32)
    inverse_rms = lax.rsqrt(jnp.mean(flat * flat, axis=1, keepdims=True) + 1e-05)
    normed = (flat * inverse_rms * norm_gain).astype(jnp.bfloat16)
    split = normed.reshape(rows, n_seq, 2, depth)

    def features(half):
        return lax.dynamic_index_in_dim(split, half, 2, keepdims=False).reshape(rows, n_seq * depth)

    normed_mine = features(stream)
    normed_other = features(1 - stream)
    span = n_seq * depth // 2
    normed_near = lax.dynamic_slice_in_dim(normed_other, core * span, span, 1)
    normed_far = lax.dynamic_slice_in_dim(normed_other, (1 - core) * span, span, 1)

    def project(mine, near, far):
        total = jnp.dot(normed_mine, mine, preferred_element_type=jnp.float32)
        total += jnp.dot(normed_near, near, preferred_element_type=jnp.float32)
        total += jnp.dot(normed_far, far, preferred_element_type=jnp.float32)
        return total.astype(jnp.bfloat16)

    keys_values = project(kv_mine, *y_share(kv_mine, core))
    partner = lax.ppermute(keys_values, "stream", [(0, 1), (1, 0)])
    kv_width = key_weight.shape[1]
    parts = 2 if kv_width % (2 * HEAD_DIM) == 0 else 1
    step = kv_width // parts
    pieces = []
    for part in range(parts):
        columns = jnp.concatenate(
            [partner[:, part * step:(part + 1) * step],
             partner[:, kv_width + part * step:kv_width + (part + 1) * step]],
            axis=1,
        )
        pieces.append(
            lax.all_gather(columns.reshape(windows, frame_count, 2 * step), "seq", axis=1, tiled=True)
        )
    queries = project(query_mine, *y_share(query_mine, core)).reshape(windows, frame_count, -1)
    out_near = out_far = None
    width = out_weight.shape[0] // 2

    repeat = query_weight.shape[1] // key_weight.shape[1]
    chunk = frame_count // ROW_CHUNKS

    def scattered(share):
        if n_tensor == 2:
            wide = share.shape[1] // 2
            away = lax.dynamic_slice_in_dim(share, (1 - tensor) * wide, wide, 1)
            kept = lax.dynamic_slice_in_dim(share, tensor * wide, wide, 1)
            came = lax.ppermute(away, "tensor", [(0, 1), (1, 0)])
            return (kept.astype(jnp.float32) + came.astype(jnp.float32)).astype(jnp.bfloat16)
        return lax.psum_scatter(share, "tensor", scatter_dimension=1, tiled=True)

    outs = []
    q_step = step * repeat
    for window in range(windows):
        early = [
            attend(
                seq * frame_count,
                queries[window][:, part * q_step:(part + 1) * q_step],
                pieces[part][window],
                repeat,
            )
            for part in range(parts - 1)
        ]
        for index in range(ROW_CHUNKS):
            low, high = index * chunk, (index + 1) * chunk
            final = attend(
                seq * frame_count + low,
                queries[window][low:high, (parts - 1) * q_step:],
                pieces[-1][window],
                repeat,
            )
            attended = jnp.concatenate([done[low:high] for done in early] + [final], axis=1)
            share_mine = jnp.dot(attended, out_mine, preferred_element_type=jnp.float32)
            if out_near is None:
                out_near, out_far, attended = y_share(out_mine, core, attended)
            attended_near = lax.dynamic_slice_in_dim(attended, core * width, width, 1)
            attended_far = lax.dynamic_slice_in_dim(attended, (1 - core) * width, width, 1)
            share_other = jnp.dot(attended_near, out_near, preferred_element_type=jnp.float32)
            share_other += jnp.dot(attended_far, out_far, preferred_element_type=jnp.float32)
            mine = scattered(share_mine.astype(jnp.bfloat16)).reshape(chunk, -1, out_half)
            other = scattered(share_other.astype(jnp.bfloat16)).reshape(chunk, -1, out_half)
            outs.append(
                jnp.where(
                    stream == 0, jnp.stack([mine, other], axis=2), jnp.stack([other, mine], axis=2)
                ).reshape(chunk, -1)
            )
    return jnp.concatenate(outs, axis=0).reshape(1, windows, frame_count, -1)


def solution(mesh):
    in_specs = (
        P("stream", None, "seq", "tensor"),
        P(),
        P("seq", "tensor"),
        P("seq", "tensor"),
        P("seq", "tensor"),
        P("tensor", "seq"),
    )
    out_specs = P("stream", None, "seq", "tensor")
    return jax.shard_map(body, mesh=mesh, in_specs=in_specs, out_specs=out_specs, check_vma=False)
```

profile of v0, /device:TPU:24, one launch (start us, length us, event | category | flops | bytes accessed | tf_op | source)
XLA Modules:
  0.0 427.3 jit_solution(7963801564547293652)
XLA Ops:
  6.5 2.0 fusion.8
  8.6 1.1 constant_dynamic-slice_fusion.9
  9.8 2.3 constant_dynamic-slice_fusion.5
  12.2 2.9 copy.11
  15.1 39.8 %all-gather.10.cloned.1.call-done = bf16[2048,1024]{1,0:T(8,128)(2,1)} async-done(((bf16[256,1024]{1,0:T(8,128)(2,1)}), bf16[2048,1024]{1,0:T(8,128)(2,1)}) %all-gather.10.cloned.1.call-update) | async-done | bytes 4194320 | tf_op jit(solution)/shard_map/all_gather | solution.py:138
  54.9 3.1 constant_dynamic-slice_fusion.6
  58.0 1.5 collective-permute-start.3
  59.5 1.5 collective-permute-start
  61.0 45.1 %collective-permute-done.3 = bf16[1024,1024]{1,0:T(8,128)(2,1)} collective-permute-done((bf16[1024,1024]{1,0:T(8,128)(2,1)}, bf16[1024,1024]{1,0:T(8,128)(2,1)}, u32[]{:S(2)}, u32[]{:S(2)}) %collective-permute-start.3) | collective-permute-done | bytes 2097184 | tf_op jit(solution)/shard_map/ppermute | solution.py:118
  106.1 1.0 collective-permute-done
  107.1 3.2 multiply_reduce_fusion
  110.3 3.1 multiply_convert_fusion
  113.4 0.3 constant_dynamic-slice_fusion.8
  113.7 2.7 copy-done.7
  116.4 2.3 fusion.32
  118.7 3.0 fusion.4
  121.7 1.4 add_convert_fusion.1
  123.1 0.4 collective-permute-start.5
  123.5 24.2 %collective-permute-done.5 = bf16[512,1024]{1,0:T(8,128)(2,1)S(1)} collective-permute-done((bf16[512,1024]{1,0:T(8,128)(2,1)S(1)}, bf16[512,1024]{1,0:T(8,128)(2,1)S(1)}, u32[]{:S(2)}, u32[]{:S(2)}) %collective-permute-start.5) | collective-permute-done | bytes 1048608 | tf_op jit(solution)/shard_map/ppermute | solution.py:179
  147.7 0.8 pad_maximum_fusion.3
  148.9 5.1 %constant_dynamic-slice_fusion.7 = bf16[1024,2048]{1,0:T(8,128)(2,1)} fusion(bf16[2048,2048]{1,0:T(8,128)(2,1)} %all-gather.8.cloned.1.call-done, s32[]{:T(128)S(6)} %select_n.86), kind=kLoop, calls=%fused_computation.56 | loop fusion | bytes 8388612 | tf_op jit(solution)/shard_map/dynamic_slice | solution.py:117
  154.0 1.4 collective-permute-start.1
  155.4 0.9 pad_maximum_fusion.4
  156.3 90.0 %collective-permute-done.1 = bf16[1024,2048]{1,0:T(8,128)(2,1)} collective-permute-done((bf16[1024,2048]{1,0:T(8,128)(2,1)}, bf16[1024,2048]{1,0:T(8,128)(2,1)}, u32[]{:S(2)}, u32[]{:S(2)}) %collective-permute-start.1) | collective-permute-done | bytes 4194336 | tf_op jit(solution)/shard_map/ppermute | solution.py:118
  246.3 5.0 %constant_dynamic-slice_fusion.3 = bf16[1024,2048]{1,0:T(8,128)(2,1)} fusion(bf16[2048,2048]{1,0:T(8,128)(2,1)} %all-gather.12.cloned.1.call-done, s32[]{:T(128)S(6)} %select_n.86), kind=kLoop, calls=%fused_computation.50 | loop fusion | bytes 8388612 | tf_op jit(solution)/shard_map/dynamic_slice | solution.py:117
  251.3 1.8 collective-permute-start.7
  253.1 7.1 %fusion.31 = f32[512,2048]{1,0:T(8,128)S(1)} fusion(bf16[512,2048]{0,1:T(8,128)(2,1)S(1)} %bitcast.31, bf16[2048,2048]{1,0:T(8,128)(2,1)} %all-gather.8.cloned.1.call-done), kind=kOutput, calls=%fused_computation.68 | convolution fusion | flops 4294967296 | bytes 14680064 | tf_op jit(solution)/shard_map/dot_general | solution.py:173
  260.2 4.7 %fusion.6 = f32[512,2048]{1,0:T(8,128)S(1)} fusion(bf16[1024,2048]{1,0:T(8,128)(2,1)} %collective-permute-done.1, bf16[512,2048]{0,1:T(8,128)(2,1)S(1)} %bitcast.28, s32[]{:T(128)S(6)} %select_n.86), kind=kOutput, calls=%fused_computation.31 | convolution fusion | flops 2147483648 | bytes 9437188 | tf_op jit(solution)/shard_map/dot_general | solution.py:174
  264.9 4.9 %add_convert_fusion = bf16[512,2048]{1,0:T(8,128)(2,1)S(1)} fusion(f32[512,2048]{1,0:T(8,128)S(1)} %fusion.31, f32[512,2048]{1,0:T(8,128)S(1)} %fusion.6, bf16[1024,2048]{1,0:T(8,128)(2,1)} %collective-permute-done.2, bf16[512,2048]{0,1:T(8,128)(2,1)S(1)} %bitcast.29, s32[]{:T(128)S(6)} %select_n.87), kind=kOutput, calls=%fused_computation.4 | convolution fusion | flops 2150629376 | bytes 15728644 | tf_op jit(solution)/shard_map/dot_general | solution.py:175
  270.0 2.2 copy-done.4
  272.2 27.4 %shard_map.64 = bf16[512,1024]{1,0:T(8,128)(2,1)S(1)} custom-call(s32[1]{0:T(128)} %bitcast.start_ref, bf16[512,1024]{1,0:T(8,128)(2,1)S(1)} %slice.36.q_ref, bf16[4096,512]{1,0:T(8,128)(2,1)S(1)} %copy-done.4, bf16[4096,512]{1,0:T(8,128)(2,1)S(1)} %copy-done.4), custom_call_target="tpu_custom_call" | custom-call | flops 17179869184 | bytes 6291456 | tf_op jit(solution)/shard_map/pallas_call | solution.py:86
  299.8 14.4 %all-gather.16.cloned.1.call-done.k_ref.v_ref = bf16[4096,512]{1,0:T(8,128)(2,1)} async-done(((bf16[512,512]{1,0:T(8,128)(2,1)}), bf16[4096,512]{1,0:T(8,128)(2,1)}) %all-gather.16.cloned.1.call-update) | async-done | bytes 4194320 | tf_op jit(solution)/shard_map/all_gather | solution.py:191
  314.2 2.2 copy-done.2
  316.4 19.1 %shard_map.65 = bf16[256,1024]{1,0:T(8,128)(2,1)S(1)} custom-call(s32[1]{0:T(128)} %bitcast.start_ref, bf16[256,1024]{1,0:T(8,128)(2,1)S(1)} %get-tuple-element.12.q_ref, bf16[4096,512]{1,0:T(8,128)(2,1)S(1)} %copy-done.2, bf16[4096,512]{1,0:T(8,128)(2,1)S(1)} %copy-done.2), custom_call_target="tpu_custom_call" | custom-call | flops 8589934592 | bytes 5242880 | tf_op jit(solution)/shard_map/pallas_call | solution.py:86
  335.5 1.1 pad_maximum_fusion.2
  336.6 8.1 %collective-permute-done.7 = bf16[1024,2048]{1,0:T(8,128)(2,1)} collective-permute-done((bf16[1024,2048]{1,0:T(8,128)(2,1)}, bf16[1024,2048]{1,0:T(8,128)(2,1)}, u32[]{:S(2)}, u32[]{:S(2)}) %collective-permute-start.7) | collective-permute-done | bytes 4194336 | tf_op jit(solution)/shard_map/ppermute | solution.py:118
  344.7 5.9 %convolution_convert_fusion.1 = bf16[256,2048]{1,0:T(8,128)(2,1)S(1)} fusion(bf16[2048,2048]{1,0:T(8,128)(2,1)} %all-gather.12.cloned.1.call-done, bf16[256,1024]{1,0:T(8,128)(2,1)S(1)} %shard_map.65, bf16[256,1024]{1,0:T(8,128)(2,1)S(1)} %get-tuple-element.14), kind=kOutput, calls=%fused_computation.10 | convolution fusion | flops 2150105088 | bytes 10485760 | tf_op jit(solution)/shard_map/dot_general | solution.py:230
  350.6 1.5 collective-permute-start.6
  352.2 18.9 %shard_map.66 = bf16[256,1024]{1,0:T(8,128)(2,1)S(1)} custom-call(s32[1]{0:T(128)} %bitcast.6.start_ref, bf16[256,1024]{1,0:T(8,128)(2,1)S(1)} %get-tuple-element.11.q_ref, bf16[4096,512]{1,0:T(8,128)(2,1)S(1)} %copy-done.3, bf16[4096,512]{1,0:T(8,128)(2,1)S(1)} %copy-done.3), custom_call_target="tpu_custom_call" | custom-call | flops 8589934592 | bytes 5242880 | tf_op jit(solution)/shard_map/pallas_call | solution.py:86
  371.1 2.3 convolution_convert_fusion
  373.5 0.6 collective-permute-start.10
  374.3 3.4 fusion.14
  377.8 3.5 fusion
  381.2 0.9 constant_dynamic-slice_fusion.2
  382.4 1.5 collective-permute-start.9
  383.8 3.5 fusion.12
  387.3 3.5 fusion.1
  390.9 0.8 constant_dynamic-slice_fusion
  391.7 0.5 collective-permute-start.11
  392.5 0.4 stack_reshape.16
  392.9 1.2 stack_reshape.18
  394.0 5.5 %collective-permute-done.9 = bf16[256,1024]{1,0:T(8,128)(2,1)S(1)} collective-permute-done((bf16[256,1024]{1,0:T(8,128)(2,1)}, bf16[256,1024]{1,0:T(8,128)(2,1)S(1)}, u32[]{:S(2)}, u32[]{:S(2)}) %collective-permute-start.9) | collective-permute-done | bytes 524320 | tf_op jit(solution)/shard_map/ppermute | solution.py:205
  399.5 1.2 add_convert_fusion.4
  400.8 0.4 stack_reshape.17
  401.2 0.8 maximum_select_fusion.2
  401.9 1.6 copy.13
  403.6 1.8 select_n.91
  405.4 4.8 %collective-permute-done.11 = bf16[256,1024]{1,0:T(8,128)(2,1)} collective-permute-done((bf16[256,1024]{1,0:T(8,128)(2,1)}, bf16[256,1024]{1,0:T(8,128)(2,1)}, u32[]{:S(2)}, u32[]{:S(2)}) %collective-permute-start.11) | collective-permute-done | bytes 524320 | tf_op jit(solution)/shard_map/ppermute | solution.py:205
  410.2 1.2 add_convert_fusion.2
  411.4 0.4 stack_reshape.19
  411.8 2.4 maximum_select_fusion.3
  414.2 1.6 copy.14
  415.8 1.6 select_n.93
  417.4 3.1 maximum_bitcast_fusion
  (55 shorter events, 1.6 us)
Async XLA Ops:
  6.5 2.1 copy-start
  6.5 48.4 %all-gather.10.cloned.1.call-start = ((), (), s32[]{:S(2)}) async-start(), calls=%async_computation.1 | async-start | bytes 4718592 | tf_op jit(solution)/shard_map/all_gather | solution.py:138
  8.6 140.3 %all-gather.8.cloned.1.call-start = ((), (), s32[]{:S(2)}) async-start(), calls=%async_computation | async-start | bytes 9437184 | tf_op jit(solution)/shard_map/all_gather | solution.py:141
  9.8 236.6 %all-gather.12.cloned.1.call-start = ((), (), s32[]{:S(2)}) async-start(), calls=%async_computation.2 | async-start | bytes 9437184 | tf_op jit(solution)/shard_map/all_gather | solution.py:144
  12.1 257.9 %all-gather.14.cloned.1.call-start = ((), (), s32[]{:S(2)}) async-start(), calls=%async_computation.3 | async-start | bytes 4718592 | tf_op jit(solution)/shard_map/all_gather | solution.py:191
  12.2 48.8 %copy-start.10 = (f32[4096]{0:T(1024)S(1)}, f32[4096]{0:T(1024)}, u32[]{:S(2)}) copy-start(f32[4096]{0:T(1024)} %param.7) | copy-start | bytes 49156
  58.0 48.1 %collective-permute-start.3 = (bf16[1024,1024]{1,0:T(8,128)(2,1)}, bf16[1024,1024]{1,0:T(8,128)(2,1)}, u32[]{:S(2)}, u32[]{:S(2)}) collective-permute-start(bf16[1024,1024]{1,0:T(8,128)(2,1)} %constant_dynamic-slice_fusion.6), channel_id=1, source_target_pairs={{0,16},{16,0},{1,17},{17,1},{2,18},{18,2},{3,19},{19,3},{4,20},{20... | collective-permute-start | bytes 6291464 | tf_op jit(solution)/shard_map/ppermute | solution.py:118
  59.5 47.6 %collective-permute-start = (bf16[512,2048]{0,1:T(8,128)(2,1)S(1)}, bf16[512,2048]{0,1:T(8,128)(2,1)}, u32[]{:S(2)}, u32[]{:S(2)}) collective-permute-start(bf16[512,2048]{0,1:T(8,128)(2,1)S(1)} %bitcast.23), channel_id=1, source_target_pairs={{0,1},{1,0},{2,3},{3,2},{4,5},{5,4},{6,7},{7,6},{8,9},{9,8},{10,11... | collective-permute-start | bytes 6291464 | tf_op jit(solution)/shard_map/ppermute | solution.py:150
  106.1 15.6 %collective-permute-start.4 = (bf16[1024,1024]{1,0:T(8,128)(2,1)}, bf16[1024,1024]{1,0:T(8,128)(2,1)S(1)}, u32[]{:S(2)}, u32[]{:S(2)}) collective-permute-start(bf16[1024,1024]{1,0:T(8,128)(2,1)} %collective-permute-done.3), channel_id=1, source_target_pairs={{0,2},{2,0},{4,6},{6,4},{8,10},{10,8},{12,14},{14,12},{1,3},{3,1},... | collective-permute-start | bytes 6291464 | tf_op jit(solution)/shard_map/ppermute | solution.py:18
  113.4 3.0 copy-start.7
  113.7 5.0 %copy-start.5 = (bf16[512,8,1,256]{0,3,2,1:T(8,128)(2,1)}, bf16[512,8,1,256]{0,3,2,1:T(8,128)(2,1)S(1)}, u32[]{:S(2)}) copy-start(bf16[512,8,1,256]{0,3,2,1:T(8,128)(2,1)S(1)} %get-tuple-element.10) | copy-start | bytes 6291460
  123.1 24.6 %collective-permute-start.5 = (bf16[512,1024]{1,0:T(8,128)(2,1)S(1)}, bf16[512,1024]{1,0:T(8,128)(2,1)S(1)}, u32[]{:S(2)}, u32[]{:S(2)}) collective-permute-start(bf16[512,1024]{1,0:T(8,128)(2,1)S(1)} %add_convert_fusion.1), channel_id=1, source_target_pairs={{0,16},{16,0},{1,17},{17,1},{2,18},{18,2},{3,19},{19,3},{4,20},{20... | collective-permute-start | bytes 3145736 | tf_op jit(solution)/shard_map/ppermute | solution.py:179
  148.6 165.6 %all-gather.16.cloned.1.call-start = ((), (), s32[]{:S(2)}) async-start(), calls=%async_computation.4 | async-start | bytes 4718592 | tf_op jit(solution)/shard_map/all_gather | solution.py:191
  154.0 92.3 %collective-permute-start.1 = (bf16[1024,2048]{1,0:T(8,128)(2,1)}, bf16[1024,2048]{1,0:T(8,128)(2,1)}, u32[]{:S(2)}, u32[]{:S(2)}) collective-permute-start(bf16[1024,2048]{1,0:T(8,128)(2,1)} %constant_dynamic-slice_fusion.7), channel_id=1, source_target_pairs={{0,16},{16,0},{1,17},{17,1},{2,18},{18,2},{3,19},{19,3},{4,20},{20... | collective-permute-start | bytes 12582920 | tf_op jit(solution)/shard_map/ppermute | solution.py:118
  246.3 18.5 %collective-permute-start.2 = (bf16[1024,2048]{1,0:T(8,128)(2,1)}, bf16[1024,2048]{1,0:T(8,128)(2,1)}, u32[]{:S(2)}, u32[]{:S(2)}) collective-permute-start(bf16[1024,2048]{1,0:T(8,128)(2,1)} %collective-permute-done.1), channel_id=1, source_target_pairs={{0,2},{2,0},{4,6},{6,4},{8,10},{10,8},{12,14},{14,12},{1,3},{3,1},... | collective-permute-start | bytes 12582920 | tf_op jit(solution)/shard_map/ppermute | solution.py:18
  246.3 6.8 %copy-start.6 = (bf16[512,8,1,256]{0,3,2,1:T(8,128)(2,1)S(1)}, bf16[512,8,1,256]{0,3,2,1:T(8,128)(2,1)}, u32[]{:S(2)}) copy-start(bf16[512,8,1,256]{0,3,2,1:T(8,128)(2,1)} %copy-done.5) | copy-start | bytes 6291460
  251.3 93.4 %collective-permute-start.7 = (bf16[1024,2048]{1,0:T(8,128)(2,1)}, bf16[1024,2048]{1,0:T(8,128)(2,1)}, u32[]{:S(2)}, u32[]{:S(2)}) collective-permute-start(bf16[1024,2048]{1,0:T(8,128)(2,1)} %constant_dynamic-slice_fusion.3), channel_id=1, source_target_pairs={{0,16},{16,0},{1,17},{17,1},{2,18},{18,2},{3,19},{19,3},{4,20},{20... | collective-permute-start | bytes 12582920 | tf_op jit(solution)/shard_map/ppermute | solution.py:118
  270.0 2.2 copy-start.4
  314.2 2.2 copy-start.2
  344.7 29.6 %collective-permute-start.8 = (bf16[1024,2048]{1,0:T(8,128)(2,1)}, bf16[1024,2048]{1,0:T(8,128)(2,1)}, u32[]{:S(2)}, u32[]{:S(2)}) collective-permute-start(bf16[1024,2048]{1,0:T(8,128)(2,1)} %collective-permute-done.7), channel_id=1, source_target_pairs={{0,2},{2,0},{4,6},{6,4},{8,10},{10,8},{12,14},{14,12},{1,3},{3,1},... | collective-permute-start | bytes 12582920 | tf_op jit(solution)/shard_map/ppermute | solution.py:18
  344.7 7.5 %copy-start.3 = (bf16[4096,512]{1,0:T(8,128)(2,1)S(1)}, bf16[4096,512]{1,0:T(8,128)(2,1)}, u32[]{:S(2)}) copy-start(bf16[4096,512]{1,0:T(8,128)(2,1)} %all-gather.16.cloned.1.call-done.k_ref.v_ref) | copy-start | bytes 12582916
  344.7 26.3 %slice-start = ((s8[8388608]{0:T(1024)(128)(4,1)}), s8[4194304]{0:T(1024)(128)(4,1)S(1)}, s32[]{:S(2)}) async-start(s8[8388608]{0:T(1024)(128)(4,1)} %bitcast.32), calls=%async_computation.5 | async-start | bytes 8388608
  350.6 23.5 %collective-permute-start.6 = (bf16[256,1024]{1,0:T(8,128)(2,1)S(1)}, bf16[256,1024]{1,0:T(8,128)(2,1)S(1)}, u32[]{:S(2)}, u32[]{:S(2)}) collective-permute-start(bf16[256,1024]{1,0:T(8,128)(2,1)S(1)} %constant_dynamic-slice_fusion.4), channel_id=1, source_target_pairs={{0,1},{1,0},{2,3},{3,2},{4,5},{5,4},{6,7},{7,6},{8,9},{9,8},{10,11... | collective-permute-start | bytes 1572872 | tf_op jit(solution)/shard_map/ppermute | solution.py:205
  352.2 18.9 %slice-start.1 = ((s8[8388608]{0:T(1024)(128)(4,1)}), s8[4194304]{0:T(1024)(128)(4,1)S(1)}, s32[]{:S(2)}) async-start(s8[8388608]{0:T(1024)(128)(4,1)} %bitcast.32), calls=%async_computation.6 | async-start | bytes 8388608
  371.1 3.2 copy-start.8
  373.5 18.8 %collective-permute-start.10 = (bf16[256,1024]{1,0:T(8,128)(2,1)S(1)}, bf16[256,1024]{1,0:T(8,128)(2,1)S(1)}, u32[]{:S(2)}, u32[]{:S(2)}) collective-permute-start(bf16[256,1024]{1,0:T(8,128)(2,1)S(1)} %constant_dynamic-slice_fusion.1), channel_id=1, source_target_pairs={{0,1},{1,0},{2,3},{3,2},{4,5},{5,4},{6,7},{7,6},{8,9},{9,8},{10,11... | collective-permute-start | bytes 1572872 | tf_op jit(solution)/shard_map/ppermute | solution.py:205
  381.2 1.1 copy-start.9
  382.4 17.2 %collective-permute-start.9 = (bf16[256,1024]{1,0:T(8,128)(2,1)}, bf16[256,1024]{1,0:T(8,128)(2,1)S(1)}, u32[]{:S(2)}, u32[]{:S(2)}) collective-permute-start(bf16[256,1024]{1,0:T(8,128)(2,1)} %constant_dynamic-slice_fusion.2), channel_id=1, source_target_pairs={{0,1},{1,0},{2,3},{3,2},{4,5},{5,4},{6,7},{7,6},{8,9},{9,8},{10,11... | collective-permute-start | bytes 1572872 | tf_op jit(solution)/shard_map/ppermute | solution.py:205
  391.7 18.4 %collective-permute-start.11 = (bf16[256,1024]{1,0:T(8,128)(2,1)}, bf16[256,1024]{1,0:T(8,128)(2,1)}, u32[]{:S(2)}, u32[]{:S(2)}) collective-permute-start(bf16[256,1024]{1,0:T(8,128)(2,1)} %constant_dynamic-slice_fusion), channel_id=1, source_target_pairs={{0,1},{1,0},{2,3},{3,2},{4,5},{5,4},{6,7},{7,6},{8,9},{9,8},{10,11... | collective-permute-start | bytes 1572872 | tf_op jit(solution)/shard_map/ppermute | solution.py:205
  411.8 8.7 %copy-start.1 = (bf16[512,2048]{1,0:T(8,128)(2,1)S(1)}, bf16[512,2048]{1,0:T(8,128)(2,1)}, u32[]{:S(2)}) copy-start(bf16[512,2048]{1,0:T(8,128)(2,1)} %param.8) | copy-start | bytes 6291460
Sparse Core Ops, SparseCore 0:
  9.0 45.9 all-gather.9
  56.5 80.2 all-gather.7
  138.4 81.6 all-gather.11
  221.5 45.2 all-gather.13
  268.3 45.8 all-gather.15
where the time goes:
time: 434 us; the launch traced here: 427 us
  waiting for transfers between devices  233 us (54%)
  Pallas kernels  65.5 us (15%)
  matrix products  45.4 us (10%)
  local copies, waits for them, and re-layouts  38.2 us (9%)
  other arithmetic  20.2 us (5%)
  between operations  13.8 us (3%)
  starting transfers between devices  11.1 us (3%)
    ppermute x3, waiting for transfers between devices, y_share(): near = lax.ppermute(part, 'stream', [(0, 1), (1, 0)])  143 us
    pallas_call x3, Pallas kernels, attend(): pl.pallas_call(functools.partial(attend_kernel, repeat), out_shape=jax.Sh...  65.5 us
    all_gather x1, waiting for transfers between devices, body(): lax.all_gather(lax.dynamic_slice_in_dim(kv_weight, stream * depth, depth,...  39.8 us
    ppermute x1, waiting for transfers between devices, body(): partner = lax.ppermute(keys_values, 'stream', [(0, 1), (1, 0)])  24.2 us
    all_gather x2, waiting for transfers between devices, body(): lax.all_gather(columns.reshape(windows, frame_count, 2 * step), 'seq', ax...  14.4 us
    dynamic_slice x3, local copies, waits for them, and re-layouts, y_share(): part = lax.dynamic_slice_in_dim(mine, core * depth, depth, 0)  13.2 us
    ppermute x4, waiting for transfers between devices, scattered(): came = lax.ppermute(away, 'tensor', [(0, 1), (1, 0)])  10.3 us
    unnamed x27, local copies, waits for them, and re-layouts  10.2 us
  transfers between devices with their start and end apart: 17, of which 9 were waited for; matrix products, arithmetic and copies ran while one was open for 20% of the time, Pallas kernels for 15%

commit v1 on v0

--- a/solution.py
+++ b/solution.py
@@ -10,6 +10,7 @@
 HEAD_DIM = 128
 ROW_CHUNKS = 2
 KEY_BLOCK = 1024
+SUBS = 4
 LOG2E = 1.4426950408889634
 
 
@@ -112,6 +113,570 @@
     )(start.reshape(1), queries, keys_values, keys_values)
 
 
+def line_order(z):
+    first = z - 1 + 2 * ((3 - z) // 3)
+    third = 3 * (1 - z // 2)
+    return (z, first, 6 - z - first - third, third)
+
+
+def remote(src, dst, send, recv, device):
+    return pltpu.make_async_remote_copy(
+        src_ref=src, dst_ref=dst, send_sem=send, recv_sem=recv, device_id=device, device_id_type=pl.DeviceIdType.MESH
+    )
+
+
+def greet(z, last, devices, up, down):
+    barrier = pltpu.get_barrier_semaphore()
+
+    def hello(device):
+        pl.semaphore_signal(barrier, inc=1, device_id=device, device_id_type=pl.DeviceIdType.MESH)
+
+    for device in devices:
+        hello(device)
+
+    @pl.when(z < last)
+    def _():
+        hello(up)
+
+    @pl.when(z > 0)
+    def _():
+        hello(down)
+
+    inner = jnp.where((z > 0) & (z < last), 1, 0)
+    pl.semaphore_wait(barrier, len(devices) + 1 + inner)
+
+
+def cross_kernel(
+    repeat, gain_ref, hidden_ref, wq_ref, wk_ref, wv_ref, wo_ref, out_ref, wo,
+    w, hid, normed, acc_ref, kv, m_ref, l_ref, came,
+    fill_sem, wo_sem, stage_sem, cross_s, cross_r, swap_s, swap_r, k_s, k_r, kc_s, kc_r,
+    wz_s, wz_r, wy_s, wy_r, wc_s, wc_r, w_own_s, w_own_r,
+    oz_s, oz_r, oy_s, oy_r, oc_s, oc_r, o_own_s, o_own_r, x_s, x_r,
+):
+    last = 3
+    c = lax.axis_index("stream")
+    s = lax.axis_index("seq")
+    t = lax.axis_index("tensor")
+    z, k = s // 2, s % 2
+    depth, q_width = wq_ref.shape
+    half = depth // 2
+    rows = half // SUBS
+    kv_width = wk_ref.shape[1]
+    frames = hid.shape[1]
+    step = frames // SUBS
+    out_depth, block = wo_ref.shape
+    out_half = out_depth // 2
+    wide = block // SUBS
+    keys = frames // SUBS
+    heads = kv_width // HEAD_DIM
+    scale = LOG2E * HEAD_DIM ** (-0.5)
+    at = {"stream": c, "seq": s, "tensor": t}
+    up, down = {**at, "seq": s + 2}, {**at, "seq": s - 2}
+    beside, mate, across = {**at, "stream": 1 - c}, {**at, "seq": 2 * z + 1 - k}, {**at, "tensor": 1 - t}
+    greet(z, last, (beside, mate, across), up, down)
+    sends = (z < last, z > 0)
+
+    def each_sub(action):
+        @pl.loop(0, SUBS)
+        def _(sub):
+            action(sub)
+
+    def source(way, hop):
+        return z - hop if way == 0 else z + hop
+
+    def arrives(way, hop):
+        return z >= hop if way == 0 else z + hop <= last
+
+    def w_part(origin, core, side, sub):
+        start = pl.multiple_of(origin * (2 * depth) + core * depth + side * half + sub * rows, rows)
+        return w.at[pl.ds(start, rows)]
+
+    def o_part(origin, core, side, sub):
+        return wo.at[2 * origin + core, sub, pl.ds(pl.multiple_of(side * out_half, out_half), out_half)]
+
+    def routes(part, z_s, z_r, y_s, y_r, c_s, c_r):
+        def along(way, hop, sub):
+            view = part(source(way, hop), k, c, sub)
+            return remote(view, view, z_s.at[way, hop, sub], z_r.at[way, hop, sub], up if way == 0 else down)
+
+        def sideways(way, hop, sub):
+            view = part(source(way, hop), k, c, sub)
+            return remote(view, view, y_s.at[way, hop - 1, sub], y_r.at[way, hop - 1, sub], beside)
+
+        def inward(way, kind, hop, sub):
+            view = part(source(way, hop), k, c if kind == 0 else 1 - c, sub)
+            return remote(view, view, c_s.at[way, kind, hop - 1, sub], c_r.at[way, kind, hop - 1, sub], mate)
+
+        def leave(way):
+            @pl.when(sends[way])
+            def _():
+                each_sub(lambda sub: along(way, 0, sub).start())
+
+        def pass_on(way, hop, sub):
+            @pl.when(arrives(way, hop))
+            def _():
+                along(way, hop - 1, sub).wait_recv()
+
+                @pl.when(sends[way] & (hop < last))
+                def _():
+                    along(way, hop, sub).start()
+
+                sideways(way, hop, sub).start()
+                inward(way, 0, hop, sub).start()
+
+        def pass_in(way, hop, sub):
+            @pl.when(arrives(way, hop))
+            def _():
+                sideways(way, hop, sub).wait_recv()
+                inward(way, 1, hop, sub).start()
+
+        def gathered(way, hop):
+            @pl.when(arrives(way, hop))
+            def _():
+                def action(sub):
+                    inward(way, 0, hop, sub).wait_recv()
+                    inward(way, 1, hop, sub).wait_recv()
+
+                each_sub(action)
+
+        def settle(sub):
+            for way in range(2):
+                for hop in range(last):
+                    @pl.when(sends[way] & arrives(way, hop))
+                    def _():
+                        along(way, hop, sub).wait_send()
+                for hop in range(1, last + 1):
+                    @pl.when(arrives(way, hop))
+                    def _():
+                        sideways(way, hop, sub).wait_send()
+                        inward(way, 0, hop, sub).wait_send()
+                        inward(way, 1, hop, sub).wait_send()
+
+        return leave, pass_on, pass_in, gathered, settle, inward
+
+    w_leave, w_on, w_in, w_gathered, w_settle, _ = routes(w_part, wz_s, wz_r, wy_s, wy_r, wc_s, wc_r)
+    o_leave, o_on, o_in, o_gathered, o_settle, o_inward = routes(o_part, oz_s, oz_r, oy_s, oy_r, oc_s, oc_r)
+
+    own = pl.multiple_of(s * depth, depth)
+    fills = [
+        pltpu.make_async_copy(wq_ref, w.at[pl.ds(own, depth), pl.ds(0, q_width)], fill_sem.at[0]),
+        pltpu.make_async_copy(wk_ref, w.at[pl.ds(own, depth), pl.ds(q_width, kv_width)], fill_sem.at[1]),
+        pltpu.make_async_copy(wv_ref, w.at[pl.ds(own, depth), pl.ds(q_width + kv_width, kv_width)], fill_sem.at[2]),
+    ]
+    mine = pltpu.make_async_copy(hidden_ref, hid.at[t], fill_sem.at[3])
+    wo_fills = [
+        pltpu.make_async_copy(wo_ref.at[:, pl.ds(sub * wide, wide)], wo.at[s, sub], wo_sem.at[sub])
+        for sub in range(SUBS)
+    ]
+
+    def crossing(piece):
+        start = pl.multiple_of(piece * step, step)
+        return remote(
+            hidden_ref.at[pl.ds(start, step)], hid.at[t, pl.ds(start, step)],
+            cross_s.at[piece], cross_r.at[piece], across,
+        )
+
+    for copy in fills:
+        copy.start()
+    mine.start()
+    each_sub(lambda piece: crossing(piece).start())
+    for copy in fills:
+        copy.wait()
+    for way in range(2):
+        w_leave(way)
+    w_block = w.at[pl.ds(own, depth)]
+    w_whole = remote(w_block, w_block, w_own_s, w_own_r, mate)
+    w_whole.start()
+    for copy in wo_fills:
+        copy.start()
+
+    tall = 16
+
+    def norm(sub):
+        crossing(sub).wait_recv()
+
+        @pl.loop(0, step // tall)
+        def _(i):
+            at_rows = pl.ds(pl.multiple_of(sub * step + i * tall, tall), tall)
+            low = hid[0, at_rows, :].astype(jnp.float32)
+            high = hid[1, at_rows, :].astype(jnp.float32)
+            total = jnp.sum(low * low, axis=1, keepdims=True) + jnp.sum(high * high, axis=1, keepdims=True)
+            inverse_rms = lax.rsqrt(total / (2 * low.shape[1]) + 1e-05)
+            part = normed.shape[2]
+            for group in range(4):
+                x = (low if group < 2 else high)[:, (group % 2) * part:(group % 2 + 1) * part]
+                gain = gain_ref[:, group * part:(group + 1) * part]
+                normed[group, at_rows, :] = (x * inverse_rms * gain).astype(jnp.bfloat16)
+
+    order = line_order(z)
+    tile = 512
+    tiles = (q_width + 2 * kv_width) // tile
+    q_tiles = q_width // tile
+    folds = frames // HEAD_DIM
+
+    def dot(place, index):
+        group = order[place]
+        columns = pl.ds(pl.multiple_of(index * tile, tile), tile)
+        return jnp.dot(
+            normed[group],
+            w[pl.ds(pl.multiple_of(group * 2 * depth, 2 * depth), 2 * depth), columns],
+            preferred_element_type=jnp.float32,
+        )
+
+    def held(index):
+        return pl.ds(index * folds, folds)
+
+    def project(place, low, high):
+        @pl.loop(low, high)
+        def _(index):
+            value = dot(place, index).reshape(folds, HEAD_DIM, tile)
+            if place == 0:
+                acc_ref[held(index)] = value
+            else:
+                acc_ref[held(index)] += value
+
+    def finish(index):
+        total = acc_ref[held(index)].reshape(frames, tile) + dot(3, index)
+        return total.astype(jnp.bfloat16)
+
+    def first_hop(sub):
+        for way in range(2):
+            w_on(way, 1, sub)
+
+    def second_hop(sub):
+        for way in range(2):
+            w_on(way, 2, sub)
+            w_in(way, 1, sub)
+        norm(sub)
+
+    each_sub(first_hop)
+    mine.wait()
+    each_sub(second_hop)
+    w_whole.wait_recv()
+    for way in range(2):
+        w_gathered(way, 1)
+    for copy in wo_fills:
+        copy.wait()
+    for sub in range(SUBS):
+        for way in range(2):
+            w_on(way, 3, sub)
+            w_in(way, 2, sub)
+        if sub == SUBS - 1:
+            for way in range(2):
+                o_leave(way)
+            o_whole = remote(wo.at[s], wo.at[s], o_own_s, o_own_r, mate)
+            o_whole.start()
+        low, high = sub * 2 * tiles // SUBS, (sub + 1) * 2 * tiles // SUBS
+        for place in range(2):
+            begin, end = max(low - place * tiles, 0), min(high - place * tiles, tiles)
+            if begin < end:
+                project(place, begin, end)
+    for way in range(2):
+        w_gathered(way, 2)
+    project(2, 0, tiles)
+    for way in range(2):
+        each_sub(lambda sub: w_in(way, 3, sub))
+        w_gathered(way, 3)
+
+    for index in range(2 * kv_width // tile):
+        hid[1, :, index * tile:(index + 1) * tile] = finish(q_tiles + index)
+
+    def key_rows(hop, sub):
+        start = pl.multiple_of((2 * (z - hop) + k) * frames + sub * keys, keys)
+        return kv.at[pl.ds(start, keys)]
+
+    def swap(sub):
+        start = pl.multiple_of(sub * keys, keys)
+        return remote(
+            hid.at[1, pl.ds(start, keys), pl.ds(0, 2 * kv_width)], key_rows(0, sub),
+            swap_s.at[sub], swap_r.at[sub], beside,
+        )
+
+    def climb(hop, sub):
+        view = key_rows(hop, sub)
+        return remote(view, view, k_s.at[hop, sub], k_r.at[hop, sub], up)
+
+    def hand(hop, sub):
+        view = key_rows(hop, sub)
+        return remote(view, view, kc_s.at[hop, sub], kc_r.at[hop, sub], mate)
+
+    def pass_keys(hop, sub):
+        @pl.when(z >= hop)
+        def _():
+            climb(hop - 1, sub).wait_recv()
+            if hop < last:
+                @pl.when(z < last)
+                def _():
+                    climb(hop, sub).start()
+            hand(hop, sub).start()
+
+    def keys_held(hop):
+        @pl.when(z >= hop)
+        def _():
+            each_sub(lambda sub: hand(hop, sub).wait_recv())
+
+    each_sub(lambda sub: swap(sub).start())
+
+    @pl.loop(0, q_tiles)
+    def _(index):
+        hid[0, :, pl.ds(pl.multiple_of(index * tile, tile), tile)] = finish(index)
+
+    def attend_to(head, start, count, masked):
+        at_keys = pl.ds(pl.multiple_of(start, count), count)
+        keys_here = kv[at_keys, pl.ds(pl.multiple_of(head * HEAD_DIM, HEAD_DIM), HEAD_DIM)]
+        values_here = kv[at_keys, pl.ds(pl.multiple_of(kv_width + head * HEAD_DIM, HEAD_DIM), HEAD_DIM)]
+        if masked:
+            allowed = lax.broadcasted_iota(jnp.int32, (count, frames), 0) <= lax.broadcasted_iota(
+                jnp.int32, (count, frames), 1
+            )
+
+        def scored(r):
+            q = hid[0, :, pl.ds(pl.multiple_of((head * repeat + r) * HEAD_DIM, HEAD_DIM), HEAD_DIM)]
+            return lax.dot_general(
+                keys_here, q, (((1,), (1,)), ((), ())), preferred_element_type=jnp.float32
+            )
+
+        following = scored(0)
+        for r in range(repeat):
+            index = head * repeat + r
+            scores = following
+            if r + 1 < repeat:
+                following = scored(r + 1)
+            if masked:
+                scores = jnp.where(allowed, scores, -1e30)
+            top = jnp.max(scores, axis=0, keepdims=True) * scale
+            before = m_ref[index]
+            fresh = jnp.maximum(before, top)
+            m_ref[index] = fresh
+            alpha = jnp.exp2(before - fresh)
+            p = jnp.exp2(scores * scale - fresh)
+            l_ref[index] = alpha * l_ref[index] + jnp.sum(p, axis=0, keepdims=True)
+            acc_ref[index] = alpha * acc_ref[index] + lax.dot_general(
+                values_here, p.astype(jnp.bfloat16), (((0,), (0,)), ((), ())), preferred_element_type=jnp.float32
+            )
+
+    def attend_own(head):
+        attend_to(head, s * frames, frames, True)
+
+        @pl.when(k == 1)
+        def _():
+            attend_to(head, (s - 1) * frames, frames, False)
+
+    def attend_hop(hop, head):
+        @pl.when(z >= hop)
+        def _():
+            attend_to(head, (z - hop) * 2 * frames, 2 * frames, False)
+
+    m_ref[...] = jnp.full_like(m_ref, -1e30)
+    l_ref[...] = jnp.zeros_like(l_ref)
+    acc_ref[...] = jnp.zeros_like(acc_ref)
+
+    def first(sub):
+        swap(sub).wait_recv()
+
+        @pl.when(z < last)
+        def _():
+            climb(0, sub).start()
+
+        hand(0, sub).start()
+        o_on(1, 1, sub)
+
+    each_sub(first)
+    keys_held(0)
+
+    for hop in range(1, last + 1):
+        def phase(sub):
+            pass_keys(hop, sub)
+            if hop < last:
+                o_on(1, hop + 1, sub)
+            o_in(1, hop, sub)
+            if hop > 1:
+                attend_hop(hop - 1, sub)
+            else:
+                attend_own(sub)
+
+        each_sub(phase)
+        keys_held(hop)
+
+    def climbed(number):
+        return number // SUBS + 1, number % SUBS
+
+    def fourth(sub):
+        o_on(0, 1, sub)
+
+        @pl.when(sub > 0)
+        def _():
+            o_in(0, 1, sub - 1)
+
+        attend_hop(last, sub)
+
+    each_sub(fourth)
+
+    w_whole.wait_send()
+    each_sub(w_settle)
+    attended = w.at[pl.ds(0, frames), pl.ds(0, q_width)]
+    stage = w.at[pl.ds(4 * frames, out_depth), pl.ds(0, 2 * wide)]
+
+    def slot_in(place, slot):
+        return w.at[pl.ds(place * frames, frames), pl.ds(pl.multiple_of(slot * 2 * wide, 2 * wide), 2 * wide)]
+
+    def kept(slot):
+        return slot_in(1, slot)
+
+    def leaving(slot):
+        return slot_in(2, slot)
+
+    def carry(slot):
+        return remote(leaving(slot), came.at[slot], x_s.at[slot], x_r.at[slot], across)
+
+    @pl.loop(0, heads)
+    def _(head):
+        for r in range(repeat):
+            index = head * repeat + r
+            out = (acc_ref[index] / l_ref[index]).T.astype(jnp.bfloat16)
+            attended[:, pl.ds(pl.multiple_of(index * HEAD_DIM, HEAD_DIM), HEAD_DIM)] = out
+
+    def shares(group, sub):
+        loads = [
+            pltpu.make_async_copy(
+                wo.at[2 * group + core, sub],
+                w.at[pl.ds(4 * frames, out_depth), pl.ds(core * wide, wide)],
+                stage_sem.at[core],
+            )
+            for core in range(2)
+        ]
+        for load in loads:
+            load.start()
+        for load in loads:
+            load.wait()
+        share = jnp.dot(attended[...], stage[...], preferred_element_type=jnp.float32).astype(jnp.bfloat16)
+        slot = (group % 2) * SUBS + sub
+
+        @pl.when(group // 2 == t)
+        def _():
+            kept(slot)[...] = share
+
+        @pl.when(group // 2 != t)
+        def _():
+            leaving(slot)[...] = share
+            carry(slot).start()
+
+    def work(number):
+        hop, sub = climbed(number)
+
+        @pl.when(arrives(0, hop))
+        def _():
+            o_inward(0, 0, hop, sub).wait_recv()
+            o_inward(0, 1, hop, sub).wait_recv()
+            shares(z - hop, sub)
+
+    o_whole.wait_recv()
+    each_sub(lambda sub: shares(z, sub))
+    for hop in range(1, last + 1):
+        o_gathered(1, hop)
+
+        @pl.when(arrives(1, hop))
+        def _():
+            each_sub(lambda sub: shares(z + hop, sub))
+
+    @pl.loop(0, SUBS - 2)
+    def _(number):
+        work(number)
+
+    @pl.loop(SUBS, last * SUBS)
+    def _(number):
+        o_on(0, *climbed(number))
+        o_in(0, *climbed(number - 1))
+        work(number - 2)
+
+    o_in(0, last, SUBS - 1)
+    work(last * SUBS - 2)
+    work(last * SUBS - 1)
+
+    high_first = z // 2
+
+    @pl.loop(0, 2 * SUBS)
+    def _(number):
+        side, sub = number // SUBS, number % SUBS
+        side = side + high_first * (1 - 2 * side)
+        slot = side * SUBS + sub
+        carry(slot).wait_recv()
+        total = (kept(slot)[...].astype(jnp.float32) + came[slot].astype(jnp.float32)).astype(jnp.bfloat16)
+        for core in range(2):
+            start = pl.multiple_of((side * 2 + core) * block + sub * wide, wide)
+            out_ref[:, pl.ds(start, wide)] = total[:, core * wide:(core + 1) * wide]
+
+    o_whole.wait_send()
+
+    @pl.loop(0, 2 * SUBS)
+    def _(slot):
+        carry(slot).wait_send()
+
+    def settle(sub):
+        crossing(sub).wait_send()
+        swap(sub).wait_send()
+        for hop in range(last + 1):
+            @pl.when(z >= hop)
+            def _():
+                hand(hop, sub).wait_send()
+                if hop < last:
+                    @pl.when(z < last)
+                    def _():
+                        climb(hop, sub).wait_send()
+        o_settle(sub)
+
+    each_sub(settle)
+
+
+def crossed(hidden, norm_gain, query_weight, key_weight, value_weight, out_weight):
+    frames, features = hidden.shape
+    depth, q_width = query_weight.shape
+    kv_width = key_weight.shape[1]
+    repeat = q_width // kv_width
+    total = q_width + 2 * kv_width
+    out_depth, block = out_weight.shape
+    wide = block // SUBS
+    count = q_width // HEAD_DIM
+    dma = pltpu.SemaphoreType.DMA
+    anywhere = pl.BlockSpec(memory_space=pl.ANY)
+    vmem = pl.BlockSpec(memory_space=pltpu.VMEM)
+    bf16, f32 = jnp.bfloat16, jnp.float32
+    line = [dma((2, 3, SUBS))] * 4 + [dma((2, 2, 3, SUBS))] * 2 + [dma] * 2
+    out, _ = pl.pallas_call(
+        functools.partial(cross_kernel, repeat),
+        out_shape=(
+            jax.ShapeDtypeStruct((frames, 4 * block), bf16),
+            jax.ShapeDtypeStruct((8, SUBS, out_depth, wide), bf16),
+        ),
+        in_specs=[vmem] + [anywhere] * 5,
+        out_specs=(vmem, anywhere),
+        scratch_shapes=[
+            pltpu.VMEM((8 * depth, total), bf16),
+            pltpu.VMEM((2, frames, features), bf16),
+            pltpu.VMEM((4, frames, features // 2), bf16),
+            pltpu.VMEM((total // HEAD_DIM, HEAD_DIM, frames), f32),
+            pltpu.VMEM((8 * frames, 2 * kv_width), bf16),
+            pltpu.VMEM((count, 1, frames), f32),
+            pltpu.VMEM((count, 1, frames), f32),
+            pltpu.VMEM((2 * SUBS, frames, 2 * wide), bf16),
+            dma((4,)), dma((SUBS,)), dma((2,)),
+            dma((SUBS,)), dma((SUBS,)), dma((SUBS,)), dma((SUBS,)),
+            dma((3, SUBS)), dma((3, SUBS)), dma((4, SUBS)), dma((4, SUBS)),
+            *line, *line,
+            dma((2 * SUBS,)), dma((2 * SUBS,)),
+        ],
+        compiler_params=pltpu.CompilerParams(
+            collective_id=0, has_side_effects=True, vmem_limit_bytes=60 * 1024 * 1024
+        ),
+        cost_estimate=pl.CostEstimate(
+            flops=16 * frames * depth * total + 16 * frames * out_depth * block,
+            bytes_accessed=4 * hidden.size,
+            transcendentals=4 * frames * frames * count,
+        ),
+    )(norm_gain.reshape(1, -1), hidden, query_weight, key_weight, value_weight, out_weight)
+    return out
+
+
 def y_share(mine, core, after=None):
     depth = mine.shape[0] // 2
     part = lax.dynamic_slice_in_dim(mine, core * depth, depth, 0)
@@ -122,7 +687,26 @@
     return near, swap_pairs(near, "seq"), after
 
 
+def fits(hidden, query_weight, key_weight):
+    meshes = (lax.axis_size("stream"), lax.axis_size("seq"), lax.axis_size("tensor"))
+    return (
+        meshes == (2, 8, 2)
+        and hidden.shape[1:] == (1, 512, 2048)
+        and query_weight.shape == (512, 2048)
+        and key_weight.shape == (512, 512)
+    )
+
+
 def body(hidden, norm_gain, query_weight, key_weight, value_projection_weight, out_weight):
+    if not fits(hidden, query_weight, key_weight):
+        return general_body(hidden, norm_gain, query_weight, key_weight, value_projection_weight, out_weight)
+    out = crossed(
+        hidden.reshape(hidden.shape[2:]), norm_gain, query_weight, key_weight, value_projection_weight, out_weight
+    )
+    return out.reshape(hidden.shape)
+
+
+def general_body(hidden, norm_gain, query_weight, key_weight, value_projection_weight, out_weight):
     windows, frame_count = hidden.shape[1], hidden.shape[2]
     n_tensor = lax.axis_size("tensor")
     n_seq = lax.axis_size("seq")

time: 434 us -> 315 us (0.73); the launches traced: 427 us -> 314 us
  Pallas kernels: 65.5 us -> 311 us
  waiting for transfers between devices: 233 us -> 0 us
  matrix products: 45.4 us -> 0 us
  local copies, waits for them, and re-layouts: 38.2 us -> 3.16 us
  other arithmetic: 20.2 us -> 0 us
  between operations: 13.8 us -> 0.01 us
  starting transfers between devices: 11.1 us -> 0 us
    pallas_call x3 -> x1, Pallas kernels: 65.5 us -> 311 us  [crossed(): pl.pallas_call(functools.partial(cross_kernel, repeat), out_shape=(jax.Sh...]
    ppermute x12 -> x0, waiting for transfers between devices: 179 us -> none  [the longest x3 143 us: y_share(): near = lax.ppermute(part, 'stream', [(0, 1), (1, 0)])]
    all_gather x5 -> x0, waiting for transfers between devices: 54.3 us -> none  [the longest x1 39.8 us: body(): lax.all_gather(lax.dynamic_slice_in_dim(kv_weight, stream * depth, depth,...]
    dot_general x12 -> x0, matrix products: 45.4 us -> none  [the longest x2 9.42 us: project(): total = jnp.dot(normed_mine, mine, preferred_element_type=jnp.float32)]
    dynamic_slice x10 -> x0, local copies, waits for them, and re-layouts: 18.7 us -> none  [the longest x3 13.2 us: y_share(): part = lax.dynamic_slice_in_dim(mine, core * depth, depth, 0)]
    ppermute x12 -> x0, starting transfers between devices: 10.8 us -> none  [the longest x3 4.67 us: y_share(): near = lax.ppermute(part, 'stream', [(0, 1), (1, 0)])]
    unnamed x27 -> x1, local copies, waits for them, and re-layouts: 10.2 us -> 3.16 us
    select_n x4 -> x0, local copies, waits for them, and re-layouts: 6.67 us -> none  [body(): jnp.where(stream == 0, jnp.stack([mine, other], axis=2), jnp.stack([other...]
  transfers between devices with their start and end apart: 17 -> 0, of which waited for: 9 -> 0; matrix products, arithmetic and copies ran while one was open for 20% -> 0% of each run, Pallas kernels for 15% -> 0%
where the time goes in v1:
time: 315 us; the launch traced here: 314 us
  Pallas kernels  311 us (99%)
  local copies, waits for them, and re-layouts  3.16 us (1%)
    pallas_call x1, Pallas kernels, crossed(): pl.pallas_call(functools.partial(cross_kernel, repeat), out_shape=(jax.Sh...  311 us

profile of v1, /device:TPU:24, one launch (start us, length us, event | category | flops | bytes accessed | tf_op | source)
XLA Modules:
  0.0 314.3 jit_solution(2278019020063687223)
XLA Ops:
  0.0 311.2 %shard_map.64 = (bf16[512,2048]{1,0:T(8,128)(2,1)}, bf16[8,4,2048,128]{3,2,1,0:T(8,128)(2,1)}) custom-call(f32[1,4096]{1,0:T(1,128)} %bitcast.5, bf16[512,2048]{1,0:T(8,128)(2,1)} %bitcast.4, bf16[512,2048]{1,0:T(8,128)(2,1)} %wq_ref.1, bf16[512,512]{1,0:T(8,128)(2,1)} %wk_ref.1, bf16[512,512]{1,0:T(8,128)(2,1)} %wv_ref.1, bf16[2048,512]{1,0:T(8,128)(2,1)} %wo_ref.1), custom_call_target="tpu_custom_call" | custom-call | flops 21474836480 | bytes 4194304 | tf_op jit(solution)/shard_map/pallas_call | solution.py:645
  311.2 3.2 %copy.8 = bf16[1,1,512,2048]{3,2,1,0:T(8,128)(2,1)} copy(bf16[1,1,512,2048]{3,2,1,0:T(8,128)(2,1)} %bitcast.3) | data formatting | bytes 4194304

commit v2 on v1

--- a/solution.py
+++ b/solution.py
@@ -167,7 +167,6 @@
     out_depth, block = wo_ref.shape
     out_half = out_depth // 2
     wide = block // SUBS
-    keys = frames // SUBS
     heads = kv_width // HEAD_DIM
     scale = LOG2E * HEAD_DIM ** (-0.5)
     at = {"stream": c, "seq": s, "tensor": t}
@@ -223,6 +222,22 @@
 
                 sideways(way, hop, sub).start()
                 inward(way, 0, hop, sub).start()
+
+        def take(way, hop, sub):
+            @pl.when(arrives(way, hop))
+            def _():
+                along(way, hop - 1, sub).wait_recv()
+                inward(way, 0, hop, sub).start()
+
+        def forward(way, hop, sub):
+            @pl.when(arrives(way, hop) & sends[way])
+            def _():
+                along(way, hop, sub).start()
+
+        def share_out(way, hop, sub):
+            @pl.when(arrives(way, hop))
+            def _():
+                sideways(way, hop, sub).start()
 
         def pass_in(way, hop, sub):
             @pl.when(arrives(way, hop))
@@ -252,10 +267,10 @@
                         inward(way, 0, hop, sub).wait_send()
                         inward(way, 1, hop, sub).wait_send()
 
-        return leave, pass_on, pass_in, gathered, settle, inward
-
-    w_leave, w_on, w_in, w_gathered, w_settle, _ = routes(w_part, wz_s, wz_r, wy_s, wy_r, wc_s, wc_r)
-    o_leave, o_on, o_in, o_gathered, o_settle, o_inward = routes(o_part, oz_s, oz_r, oy_s, oy_r, oc_s, oc_r)
+        return leave, pass_on, pass_in, gathered, settle, inward, (take, forward, share_out)
+
+    w_leave, w_on, w_in, w_gathered, w_settle, *_ = routes(w_part, wz_s, wz_r, wy_s, wy_r, wc_s, wc_r)
+    o_leave, o_on, o_in, _, o_settle, o_inward, (o_take, o_forward, o_out) = routes(o_part, oz_s, oz_r, oy_s, oy_r, oc_s, oc_r)
 
     own = pl.multiple_of(s * depth, depth)
     fills = [
@@ -379,17 +394,20 @@
         w_gathered(way, 3)
 
     for index in range(2 * kv_width // tile):
-        hid[1, :, index * tile:(index + 1) * tile] = finish(q_tiles + index)
-
-    def key_rows(hop, sub):
-        start = pl.multiple_of((2 * (z - hop) + k) * frames + sub * keys, keys)
-        return kv.at[pl.ds(start, keys)]
-
-    def swap(sub):
-        start = pl.multiple_of(sub * keys, keys)
+        piece = finish(q_tiles + index)
+        for head in range(heads):
+            start = (2 * head + index) * HEAD_DIM
+            hid[1, :, start:start + HEAD_DIM] = piece[:, head * HEAD_DIM:(head + 1) * HEAD_DIM]
+
+    def key_rows(hop, head):
+        start = pl.multiple_of((2 * (z - hop) + k) * frames, frames)
+        return kv.at[head, pl.ds(start, frames)]
+
+    def swap(head):
+        start = pl.multiple_of(head * 2 * HEAD_DIM, 2 * HEAD_DIM)
         return remote(
-            hid.at[1, pl.ds(start, keys), pl.ds(0, 2 * kv_width)], key_rows(0, sub),
-            swap_s.at[sub], swap_r.at[sub], beside,
+            hid.at[1, pl.ds(0, frames), pl.ds(start, 2 * HEAD_DIM)], key_rows(0, head),
+            swap_s.at[head], swap_r.at[head], beside,
         )
 
     def climb(hop, sub):
@@ -410,11 +428,6 @@
                     climb(hop, sub).start()
             hand(hop, sub).start()
 
-    def keys_held(hop):
-        @pl.when(z >= hop)
-        def _():
-            each_sub(lambda sub: hand(hop, sub).wait_recv())
-
     each_sub(lambda sub: swap(sub).start())
 
     @pl.loop(0, q_tiles)
@@ -423,8 +436,8 @@
 
     def attend_to(head, start, count, masked):
         at_keys = pl.ds(pl.multiple_of(start, count), count)
-        keys_here = kv[at_keys, pl.ds(pl.multiple_of(head * HEAD_DIM, HEAD_DIM), HEAD_DIM)]
-        values_here = kv[at_keys, pl.ds(pl.multiple_of(kv_width + head * HEAD_DIM, HEAD_DIM), HEAD_DIM)]
+        keys_here = kv[head, at_keys, 0:HEAD_DIM]
+        values_here = kv[head, at_keys, HEAD_DIM:2 * HEAD_DIM]
         if masked:
             allowed = lax.broadcasted_iota(jnp.int32, (count, frames), 0) <= lax.broadcasted_iota(
                 jnp.int32, (count, frames), 1
@@ -456,6 +469,7 @@
             )
 
     def attend_own(head):
+        hand(0, head).wait_recv()
         attend_to(head, s * frames, frames, True)
 
         @pl.when(k == 1)
@@ -465,6 +479,7 @@
     def attend_hop(hop, head):
         @pl.when(z >= hop)
         def _():
+            hand(hop, head).wait_recv()
             attend_to(head, (z - hop) * 2 * frames, 2 * frames, False)
 
     m_ref[...] = jnp.full_like(m_ref, -1e30)
@@ -479,43 +494,63 @@
             climb(0, sub).start()
 
         hand(0, sub).start()
-        o_on(1, 1, sub)
+        o_take(1, 1, sub)
+        o_forward(1, 1, sub)
+
+        @pl.when(sub > 0)
+        def _():
+            attend_own(sub - 1)
 
     each_sub(first)
-    keys_held(0)
-
-    for hop in range(1, last + 1):
-        def phase(sub):
-            pass_keys(hop, sub)
-            if hop < last:
-                o_on(1, hop + 1, sub)
-            o_in(1, hop, sub)
-            if hop > 1:
-                attend_hop(hop - 1, sub)
+
+    def catch_up(hop, sub):
+        @pl.when(sub > 0)
+        def _():
+            attend_hop(hop, sub - 1)
+
+        @pl.when(sub == 0)
+        def _():
+            if hop == 1:
+                attend_own(heads - 1)
             else:
-                attend_own(sub)
-
-        each_sub(phase)
-        keys_held(hop)
+                attend_hop(hop - 1, heads - 1)
+
+    def phase_1(sub):
+        pass_keys(1, sub)
+        o_take(1, 2, sub)
+        o_forward(1, 2, sub)
+        o_take(0, 1, sub)
+        o_out(1, 1, sub)
+        o_out(0, 1, sub)
+        catch_up(1, sub)
+
+    def phase_2(sub):
+        pass_keys(2, sub)
+        o_take(1, 3, sub)
+        o_out(1, 2, sub)
+        catch_up(2, sub)
+
+    def phase_3(sub):
+        o_forward(0, 1, sub)
+        pass_keys(3, sub)
+        o_out(1, 3, sub)
+        o_in(1, 1, sub)
+        o_in(0, 1, sub)
+        catch_up(3, sub)
+
+    each_sub(phase_1)
+    each_sub(phase_2)
+    each_sub(phase_3)
+    attend_hop(3, heads - 1)
+    each_sub(lambda sub: o_in(1, 2, sub))
+    each_sub(lambda sub: o_in(1, 3, sub))
 
     def climbed(number):
         return number // SUBS + 1, number % SUBS
-
-    def fourth(sub):
-        o_on(0, 1, sub)
-
-        @pl.when(sub > 0)
-        def _():
-            o_in(0, 1, sub - 1)
-
-        attend_hop(last, sub)
-
-    each_sub(fourth)
 
     w_whole.wait_send()
     each_sub(w_settle)
     attended = w.at[pl.ds(0, frames), pl.ds(0, q_width)]
-    stage = w.at[pl.ds(4 * frames, out_depth), pl.ds(0, 2 * wide)]
 
     def slot_in(place, slot):
         return w.at[pl.ds(place * frames, frames), pl.ds(pl.multiple_of(slot * 2 * wide, 2 * wide), 2 * wide)]
@@ -536,20 +571,39 @@
             out = (acc_ref[index] / l_ref[index]).T.astype(jnp.bfloat16)
             attended[:, pl.ds(pl.multiple_of(index * HEAD_DIM, HEAD_DIM), HEAD_DIM)] = out
 
-    def shares(group, sub):
-        loads = [
-            pltpu.make_async_copy(
-                wo.at[2 * group + core, sub],
-                w.at[pl.ds(4 * frames, out_depth), pl.ds(core * wide, wide)],
-                stage_sem.at[core],
-            )
-            for core in range(2)
-        ]
-        for load in loads:
-            load.start()
-        for load in loads:
-            load.wait()
-        share = jnp.dot(attended[...], stage[...], preferred_element_type=jnp.float32).astype(jnp.bfloat16)
+    def which(task):
+        place, sub = task // SUBS, task % SUBS
+        return place, sub, place <= last - z
+
+    def ready(task):
+        place, sub, above = which(task)
+
+        @pl.when(above & (place > 0))
+        def _():
+            for kind in range(2):
+                o_inward(1, kind, place, sub).wait_recv()
+
+        @pl.when(place > last - z)
+        def _():
+            for kind in range(2):
+                o_inward(0, kind, place - (last - z), sub).wait_recv()
+
+    def load(task, buffer, core):
+        place, sub, above = which(task)
+        group = jnp.where(above, z + place, last - place)
+        return pltpu.make_async_copy(
+            wo.at[2 * group + core, sub],
+            w.at[pl.ds(4 * frames, out_depth), pl.ds((2 * buffer + core) * wide, wide)],
+            stage_sem.at[buffer, core],
+        )
+
+    def shares(task, buffer):
+        place, sub, above = which(task)
+        group = jnp.where(above, z + place, last - place)
+        for core in range(2):
+            load(task, buffer, core).wait()
+        weights = w[4 * frames:4 * frames + out_depth, 2 * buffer * wide:2 * (buffer + 1) * wide]
+        share = jnp.dot(attended[...], weights, preferred_element_type=jnp.float32).astype(jnp.bfloat16)
         slot = (group % 2) * SUBS + sub
 
         @pl.when(group // 2 == t)
@@ -561,37 +615,32 @@
             leaving(slot)[...] = share
             carry(slot).start()
 
-    def work(number):
-        hop, sub = climbed(number)
-
-        @pl.when(arrives(0, hop))
-        def _():
-            o_inward(0, 0, hop, sub).wait_recv()
-            o_inward(0, 1, hop, sub).wait_recv()
-            shares(z - hop, sub)
+    def work(*tasks):
+        for buffer, task in enumerate(tasks):
+            ready(task)
+            for core in range(2):
+                load(task, buffer, core).start()
+        for buffer, task in enumerate(tasks):
+            shares(task, buffer)
 
     o_whole.wait_recv()
-    each_sub(lambda sub: shares(z, sub))
-    for hop in range(1, last + 1):
-        o_gathered(1, hop)
-
-        @pl.when(arrives(1, hop))
-        def _():
-            each_sub(lambda sub: shares(z + hop, sub))
-
-    @pl.loop(0, SUBS - 2)
-    def _(number):
-        work(number)
-
-    @pl.loop(SUBS, last * SUBS)
-    def _(number):
+
+    @pl.loop(0, 2 * SUBS - 1)
+    def _(pair):
+        number = pair + SUBS
         o_on(0, *climbed(number))
-        o_in(0, *climbed(number - 1))
-        work(number - 2)
-
+
+        @pl.when(pair > 0)
+        def _():
+            o_in(0, *climbed(number - 1))
+
+        work(2 * pair, 2 * pair + 1)
+
+    o_on(0, last, SUBS - 1)
+    o_in(0, last, SUBS - 2)
+    work(4 * SUBS - 2)
     o_in(0, last, SUBS - 1)
-    work(last * SUBS - 2)
-    work(last * SUBS - 1)
+    work(4 * SUBS - 1)
 
     high_first = z // 2
 
@@ -655,11 +704,11 @@
             pltpu.VMEM((2, frames, features), bf16),
             pltpu.VMEM((4, frames, features // 2), bf16),
             pltpu.VMEM((total // HEAD_DIM, HEAD_DIM, frames), f32),
-            pltpu.VMEM((8 * frames, 2 * kv_width), bf16),
+            pltpu.VMEM((kv_width // HEAD_DIM, 8 * frames, 2 * HEAD_DIM), bf16),
             pltpu.VMEM((count, 1, frames), f32),
             pltpu.VMEM((count, 1, frames), f32),
             pltpu.VMEM((2 * SUBS, frames, 2 * wide), bf16),
-            dma((4,)), dma((SUBS,)), dma((2,)),
+            dma((4,)), dma((SUBS,)), dma((2, 2)),
             dma((SUBS,)), dma((SUBS,)), dma((SUBS,)), dma((SUBS,)),
             dma((3, SUBS)), dma((3, SUBS)), dma((4, SUBS)), dma((4, SUBS)),
             *line, *line,

time: 315 us -> 296 us (0.940)
  Pallas kernels: 311 us -> 292 us
    pallas_call x1, Pallas kernels: 311 us -> 292 us  [crossed(): pl.pallas_call(functools.partial(cross_kernel, repeat), out_shape=(jax.Sh...]
where the time goes in v2:
time: 296 us; the launch traced here: 295 us
  Pallas kernels  292 us (99%)
  local copies, waits for them, and re-layouts  3.16 us (1%)
    pallas_call x1, Pallas kernels, crossed(): pl.pallas_call(functools.partial(cross_kernel, repeat), out_shape=(jax.Sh...  292 us

profile of v2, /device:TPU:24, one launch (start us, length us, event | category | flops | bytes accessed | tf_op | source)
XLA Modules:
  0.0 295.3 jit_solution(11439741172913365176)
XLA Ops:
  0.0 292.1 %shard_map.64 = (bf16[512,2048]{1,0:T(8,128)(2,1)}, bf16[8,4,2048,128]{3,2,1,0:T(8,128)(2,1)}) custom-call(f32[1,4096]{1,0:T(1,128)} %bitcast.5, bf16[512,2048]{1,0:T(8,128)(2,1)} %bitcast.4, bf16[512,2048]{1,0:T(8,128)(2,1)} %wq_ref.1, bf16[512,512]{1,0:T(8,128)(2,1)} %wk_ref.1, bf16[512,512]{1,0:T(8,128)(2,1)} %wv_ref.1, bf16[2048,512]{1,0:T(8,128)(2,1)} %wo_ref.1), custom_call_target="tpu_custom_call" | custom-call | flops 21474836480 | bytes 4194304 | tf_op jit(solution)/shard_map/pallas_call | solution.py:694
  292.1 3.2 %copy.8 = bf16[1,1,512,2048]{3,2,1,0:T(8,128)(2,1)} copy(bf16[1,1,512,2048]{3,2,1,0:T(8,128)(2,1)} %bitcast.3) | data formatting | bytes 4194304

commit v3 on v2

--- a/solution.py
+++ b/solution.py
@@ -254,10 +254,20 @@
 
                 each_sub(action)
 
-        def settle(sub):
+        def final_hop(way):
+            return z if way == 0 else last - z
+
+        def drained(way):
+            @pl.when(sends[way])
+            def _():
+                along(way, final_hop(way), SUBS - 1).wait_send()
+
+        def settle(sub, seen=False):
             for way in range(2):
                 for hop in range(last):
-                    @pl.when(sends[way] & arrives(way, hop))
+                    unseen = jnp.logical_not((final_hop(way) == hop) & (sub == SUBS - 1)) if seen else True
+
+                    @pl.when(sends[way] & arrives(way, hop) & unseen)
                     def _():
                         along(way, hop, sub).wait_send()
                 for hop in range(1, last + 1):
@@ -267,10 +277,10 @@
                         inward(way, 0, hop, sub).wait_send()
                         inward(way, 1, hop, sub).wait_send()
 
-        return leave, pass_on, pass_in, gathered, settle, inward, (take, forward, share_out)
-
-    w_leave, w_on, w_in, w_gathered, w_settle, *_ = routes(w_part, wz_s, wz_r, wy_s, wy_r, wc_s, wc_r)
-    o_leave, o_on, o_in, _, o_settle, o_inward, (o_take, o_forward, o_out) = routes(o_part, oz_s, oz_r, oy_s, oy_r, oc_s, oc_r)
+        return leave, pass_on, pass_in, gathered, settle, inward, (take, forward, share_out), drained
+
+    w_leave, w_on, w_in, w_gathered, w_settle, _, _, w_drained = routes(w_part, wz_s, wz_r, wy_s, wy_r, wc_s, wc_r)
+    o_leave, o_on, o_in, _, o_settle, o_inward, (o_take, o_forward, o_out), _ = routes(o_part, oz_s, oz_r, oy_s, oy_r, oc_s, oc_r)
 
     own = pl.multiple_of(s * depth, depth)
     fills = [
@@ -375,12 +385,10 @@
     for sub in range(SUBS):
         for way in range(2):
             w_on(way, 3, sub)
+            if sub == SUBS - 1:
+                w_drained(way)
+                o_leave(way)
             w_in(way, 2, sub)
-        if sub == SUBS - 1:
-            for way in range(2):
-                o_leave(way)
-            o_whole = remote(wo.at[s], wo.at[s], o_own_s, o_own_r, mate)
-            o_whole.start()
         low, high = sub * 2 * tiles // SUBS, (sub + 1) * 2 * tiles // SUBS
         for place in range(2):
             begin, end = max(low - place * tiles, 0), min(high - place * tiles, tiles)
@@ -388,6 +396,8 @@
                 project(place, begin, end)
     for way in range(2):
         w_gathered(way, 2)
+    o_whole = remote(wo.at[s], wo.at[s], o_own_s, o_own_r, mate)
+    o_whole.start()
     project(2, 0, tiles)
     for way in range(2):
         each_sub(lambda sub: w_in(way, 3, sub))
@@ -549,7 +559,7 @@
         return number // SUBS + 1, number % SUBS
 
     w_whole.wait_send()
-    each_sub(w_settle)
+    each_sub(lambda sub: w_settle(sub, True))
     attended = w.at[pl.ds(0, frames), pl.ds(0, q_width)]
 
     def slot_in(place, slot):
@@ -571,26 +581,42 @@
             out = (acc_ref[index] / l_ref[index]).T.astype(jnp.bfloat16)
             attended[:, pl.ds(pl.multiple_of(index * HEAD_DIM, HEAD_DIM), HEAD_DIM)] = out
 
+    orders = [
+        [[2, 3, 0, 1], [0, 1, 2, 3]],
+        [[2, 3, 1, 0], [1, 0, 2, 3]],
+        [[2, 3, 1, 0], [1, 2, 0, 3]],
+        [[3, 2, 1, 0], [3, 2, 1, 0]],
+    ]
+    turns = []
+    for place in range(4):
+        group = 0
+        for plane in range(4):
+            for side in range(2):
+                group = jnp.where((z == plane) & (t == side), orders[plane][side][place], group)
+        turns.append(group)
+
     def which(task):
         place, sub = task // SUBS, task % SUBS
-        return place, sub, place <= last - z
+        group = turns[3]
+        for index in range(3):
+            group = jnp.where(place == index, turns[index], group)
+        return group, sub
 
     def ready(task):
-        place, sub, above = which(task)
-
-        @pl.when(above & (place > 0))
+        group, sub = which(task)
+
+        @pl.when(group > z)
         def _():
             for kind in range(2):
-                o_inward(1, kind, place, sub).wait_recv()
-
-        @pl.when(place > last - z)
+                o_inward(1, kind, group - z, sub).wait_recv()
+
+        @pl.when(group < z)
         def _():
             for kind in range(2):
-                o_inward(0, kind, place - (last - z), sub).wait_recv()
+                o_inward(0, kind, z - group, sub).wait_recv()
 
     def load(task, buffer, core):
-        place, sub, above = which(task)
-        group = jnp.where(above, z + place, last - place)
+        group, sub = which(task)
         return pltpu.make_async_copy(
             wo.at[2 * group + core, sub],
             w.at[pl.ds(4 * frames, out_depth), pl.ds((2 * buffer + core) * wide, wide)],
@@ -598,8 +624,7 @@
         )
 
     def shares(task, buffer):
-        place, sub, above = which(task)
-        group = jnp.where(above, z + place, last - place)
+        group, sub = which(task)
         for core in range(2):
             load(task, buffer, core).wait()
         weights = w[4 * frames:4 * frames + out_depth, 2 * buffer * wide:2 * (buffer + 1) * wide]
@@ -625,6 +650,14 @@
 
     o_whole.wait_recv()
 
+    relay = z == 2
+
+    @pl.when(jnp.logical_not(relay))
+    def _():
+        @pl.loop(0, SUBS - 1)
+        def _(pair):
+            work(2 * pair, 2 * pair + 1)
+
     @pl.loop(0, 2 * SUBS - 1)
     def _(pair):
         number = pair + SUBS
@@ -634,15 +667,26 @@
         def _():
             o_in(0, *climbed(number - 1))
 
-        work(2 * pair, 2 * pair + 1)
+        @pl.when(relay)
+        def _():
+            work(2 * pair, 2 * pair + 1)
+
+        @pl.when(jnp.logical_not(relay))
+        def _():
+            work(2 * SUBS - 2 + pair)
 
     o_on(0, last, SUBS - 1)
     o_in(0, last, SUBS - 2)
+
+    @pl.when(jnp.logical_not(relay))
+    def _():
+        work(4 * SUBS - 3)
+
     work(4 * SUBS - 2)
     o_in(0, last, SUBS - 1)
     work(4 * SUBS - 1)
 
-    high_first = z // 2
+    high_first = jnp.where(z > 2 * t, 1, 0)
 
     @pl.loop(0, 2 * SUBS)
     def _(number):

time: 296 us -> 290 us (0.980)
  Pallas kernels: 292 us -> 287 us
    pallas_call x1, Pallas kernels: 292 us -> 287 us  [crossed(): pl.pallas_call(functools.partial(cross_kernel, repeat), out_shape=(jax.Sh...]
where the time goes in v3:
time: 290 us
  Pallas kernels  287 us (99%)
  local copies, waits for them, and re-layouts  3.16 us (1%)
    pallas_call x1, Pallas kernels, crossed(): pl.pallas_call(functools.partial(cross_kernel, repeat), out_shape=(jax.Sh...  287 us

profile of v3, /device:TPU:24, one launch (start us, length us, event | category | flops | bytes accessed | tf_op | source)
XLA Modules:
  0.0 289.9 jit_solution(7595749628977008797)
XLA Ops:
  0.0 286.7 %shard_map.64 = (bf16[512,2048]{1,0:T(8,128)(2,1)}, bf16[8,4,2048,128]{3,2,1,0:T(8,128)(2,1)}) custom-call(f32[1,4096]{1,0:T(1,128)} %bitcast.5, bf16[512,2048]{1,0:T(8,128)(2,1)} %bitcast.4, bf16[512,2048]{1,0:T(8,128)(2,1)} %wq_ref.1, bf16[512,512]{1,0:T(8,128)(2,1)} %wk_ref.1, bf16[512,512]{1,0:T(8,128)(2,1)} %wv_ref.1, bf16[2048,512]{1,0:T(8,128)(2,1)} %wo_ref.1), custom_call_target="tpu_custom_call" | custom-call | flops 21474836480 | bytes 4194304 | tf_op jit(solution)/shard_map/pallas_call | solution.py:738
  286.7 3.2 %copy.8 = bf16[1,1,512,2048]{3,2,1,0:T(8,128)(2,1)} copy(bf16[1,1,512,2048]{3,2,1,0:T(8,128)(2,1)} %bitcast.3) | data formatting | bytes 4194304

commit v4 on v3

--- a/solution.py
+++ b/solution.py
@@ -552,12 +552,12 @@
     each_sub(phase_2)
     each_sub(phase_3)
     attend_hop(3, heads - 1)
-    each_sub(lambda sub: o_in(1, 2, sub))
-    each_sub(lambda sub: o_in(1, 3, sub))
 
     def climbed(number):
         return number // SUBS + 1, number % SUBS
 
+    o_on(0, 2, 0)
+    o_on(0, 2, 1)
     w_whole.wait_send()
     each_sub(lambda sub: w_settle(sub, True))
     attended = w.at[pl.ds(0, frames), pl.ds(0, q_width)]
@@ -586,6 +586,10 @@
         [[2, 3, 1, 0], [1, 0, 2, 3]],
         [[2, 3, 1, 0], [1, 2, 0, 3]],
         [[3, 2, 1, 0], [3, 2, 1, 0]],
+    ]
+    blend = [
+        (3, 0), (3, 1), (1, 0), (1, 1), (3, 2), (1, 2), (1, 3), (3, 3),
+        (2, 0), (0, 0), (0, 1), (2, 1), (0, 2), (2, 2), (2, 3), (0, 3),
     ]
     turns = []
     for place in range(4):
@@ -600,6 +604,11 @@
         group = turns[3]
         for index in range(3):
             group = jnp.where(place == index, turns[index], group)
+        mixed = (z == last) & (t == 1)
+        for index, (plane, piece) in enumerate(blend):
+            here = mixed & (task == index)
+            group = jnp.where(here, plane, group)
+            sub = jnp.where(here, piece, sub)
         return group, sub
 
     def ready(task):
@@ -650,37 +659,25 @@
 
     o_whole.wait_recv()
 
-    relay = z == 2
-
-    @pl.when(jnp.logical_not(relay))
-    def _():
-        @pl.loop(0, SUBS - 1)
-        def _(pair):
-            work(2 * pair, 2 * pair + 1)
-
-    @pl.loop(0, 2 * SUBS - 1)
-    def _(pair):
-        number = pair + SUBS
-        o_on(0, *climbed(number))
-
-        @pl.when(pair > 0)
-        def _():
-            o_in(0, *climbed(number - 1))
-
-        @pl.when(relay)
-        def _():
-            work(2 * pair, 2 * pair + 1)
-
-        @pl.when(jnp.logical_not(relay))
-        def _():
-            work(2 * SUBS - 2 + pair)
-
-    o_on(0, last, SUBS - 1)
-    o_in(0, last, SUBS - 2)
-
-    @pl.when(jnp.logical_not(relay))
-    def _():
-        work(4 * SUBS - 3)
+    o_on(0, 2, 2)
+    o_in(1, 2, 0)
+    o_in(1, 2, 1)
+    work(0, 1)
+    o_on(0, 2, 3)
+    o_in(0, 2, 0)
+    o_in(0, 2, 1)
+    o_in(1, 2, 2)
+    o_in(1, 2, 3)
+    work(2, 3)
+    o_in(0, 2, 2)
+    each_sub(lambda sub: o_in(1, 3, sub))
+    work(4, 5)
+
+    @pl.loop(0, SUBS)
+    def _(sub):
+        o_on(0, last, sub)
+        o_in(0, *climbed(2 * SUBS - 1 + sub))
+        work(6 + 2 * sub, 7 + 2 * sub)
 
     work(4 * SUBS - 2)
     o_in(0, last, SUBS - 1)

time: 290 us -> 285 us (0.983)
  Pallas kernels: 287 us -> 279 us
    pallas_call x1, Pallas kernels: 287 us -> 279 us  [crossed(): pl.pallas_call(functools.partial(cross_kernel, repeat), out_shape=(jax.Sh...]
where the time goes in v4:
time: 285 us; the launch traced here: 283 us
  Pallas kernels  279 us (98%)
  local copies, waits for them, and re-layouts  3.16 us (1%)
    pallas_call x1, Pallas kernels, crossed(): pl.pallas_call(functools.partial(cross_kernel, repeat), out_shape=(jax.Sh...  279 us

profile of v4, /device:TPU:24, one launch (start us, length us, event | category | flops | bytes accessed | tf_op | source)
XLA Modules:
  0.0 282.6 jit_solution(6165912110722998402)
XLA Ops:
  0.0 279.0 %shard_map.64 = (bf16[512,2048]{1,0:T(8,128)(2,1)}, bf16[8,4,2048,128]{3,2,1,0:T(8,128)(2,1)}) custom-call(f32[1,4096]{1,0:T(1,128)} %bitcast.5, bf16[512,2048]{1,0:T(8,128)(2,1)} %bitcast.4, bf16[512,2048]{1,0:T(8,128)(2,1)} %wq_ref.1, bf16[512,512]{1,0:T(8,128)(2,1)} %wk_ref.1, bf16[512,512]{1,0:T(8,128)(2,1)} %wv_ref.1, bf16[2048,512]{1,0:T(8,128)(2,1)} %wo_ref.1), custom_call_target="tpu_custom_call" | custom-call | flops 21474836480 | bytes 4194304 | tf_op jit(solution)/shard_map/pallas_call | solution.py:735
  279.0 3.2 %copy.8 = bf16[1,1,512,2048]{3,2,1,0:T(8,128)(2,1)} copy(bf16[1,1,512,2048]{3,2,1,0:T(8,128)(2,1)} %bitcast.3) | data formatting | bytes 4194304
